TPU v7x, 32 devices: a whole 2x2x4 slice. The times are simulated.
32 devices in a mesh: groups: 2 (over y), cube: 4 (over z), row: 2 (over x), pair: 2 (over core).
Axes of the slice: x: 2, y: 2, z: 4, core: 2. Of those that a mesh axis runs over, the one named last changes fastest.
Arguments:
- ligand: float32 [2, 64, 32, 1024], P('pair', ('groups', 'cube', 'row')), parts along dimension 1, may hold values from 0.05 to 3
- density: int32 [64, 32, 1024], P(('groups', 'cube', 'row')), parts along dimension 0, may hold values from 0 to 7
- counts: int32 [16], P(('groups', 'cube', 'row')), parts along dimension 0, may hold values from 1 to 4, as said below
- neighbours: int32 [64, 6], P(('groups', 'cube', 'row')), parts along dimension 0, may hold values from -1 to 31, as said below
- diffusion: float32 [2], replicated, may hold values from 0.04 to 0.14
- uptake: float32 [2], replicated, may hold values from 0.03 to 0.18
Outputs:
- ligand_out: float32 [2, 64, 32, 1024], P('pair', ('groups', 'cube', 'row')), parts along dimension 1
There are 2 independent parts, one for each index of `groups`. A program takes and returns all parts, laid end to end along the dimension named above; an argument that names none is the same for every part. Nothing has to cross between parts.
Inputs may be any that keep to these rules, and one draw needn't show every extreme that they name: `counts`: the number of occupied tiles of each block of 4 slots; they fill the first slots of their block; some block is full and some block holds 1. Block b = layer * 2 + band holds tile slots b * 4 to (b + 1) * 4 - 1; an entry is -1 for an empty slot, for a face on the volume's boundary and for an unoccupied place; x neighbours lie in the same block, a -y neighbour in block b or b - 1, a +y neighbour in block b or b + 1, a -z neighbour in block b - 2, a +z neighbour in block b + 2; if tile u names v across a face, v names u across the opposite face.
All inputs are finite; a program needn't handle non-finite values.
Results may differ from a plain program's by a relative error of at most 0.00007.
Values sent between devices are 32-bit elements; how exact they have to be, the bound alone decides.
A program may use at most 64 MiB of HBM per device.

v0:
```python
import jax
import jax.numpy as jnp
from jax import lax
from jax.sharding import PartitionSpec as P

EX = 32
EY = 32
STEPS = 4


def with_halo(cells, sides, width):
    for axis, dim in sides:
        count = lax.axis_size(axis)
        ends = count - 1
        head = lax.slice_in_dim(cells, 0, width, axis=dim)
        tail = lax.slice_in_dim(cells, cells.shape[dim] - width, cells.shape[dim], axis=dim)
        cells = jnp.concatenate(
            [
                lax.ppermute(tail, axis, [(i, (i + 1) % count) for i in range(ends)]),
                cells,
                lax.ppermute(head, axis, [((i + 1) % count, i) for i in range(ends)]),
            ],
            axis=dim,
        )
    return cells


def from_partner(value, axis, distance):
    mask = 2**distance
    pairs = [(source, source ^ mask) for source in range(lax.axis_size(axis))]
    return lax.ppermute(value, axis, pairs)


def gather_faces(faces, index, okay):
    count = faces.shape[1]
    slot_ids = jnp.arange(count, dtype=jnp.int32)
    select = jnp.where(
        okay[:, None] & (index[:, None] == slot_ids[None, :]), jnp.float32(1.0), jnp.float32(0.0)
    )
    return jnp.einsum("ts,ksf->ktf", select, faces, precision=lax.Precision.HIGHEST)


def face_tables(cells):
    position = jnp.arange(cells, dtype=jnp.int32)[:, None]
    column = jnp.arange(EX, dtype=jnp.int32)[None, :]
    pick_low = jnp.where(position == column * EY, jnp.float32(1.0), jnp.float32(0.0))
    pick_high = jnp.where(position == column * EY + EY - 1, jnp.float32(1.0), jnp.float32(0.0))
    return (pick_low, pick_high)


def neighbour_sum(field, below, above, neighbours, block):
    kinds, slots, depth, cells = field.shape
    base = block * slots
    pick_low, pick_high = face_tables(cells)
    x_low = field[..., :EY].reshape(kinds, slots, -1)
    x_high = field[..., cells - EY :].reshape(kinds, slots, -1)
    y_low4 = jnp.einsum("ksdc,cx->ksdx", field, pick_low, precision=lax.Precision.HIGHEST)
    y_high4 = jnp.einsum("ksdc,cx->ksdx", field, pick_high, precision=lax.Precision.HIGHEST)
    y_low = y_low4.reshape(kinds, slots, -1)
    y_high = y_high4.reshape(kinds, slots, -1)
    left = neighbours[:, 0]
    right = neighbours[:, 1]
    front = neighbours[:, 2]
    back = neighbours[:, 3]
    ghost_left = gather_faces(x_high, left - base, left >= 0).reshape(kinds, slots, depth, EY)
    ghost_right = gather_faces(x_low, right - base, right >= 0).reshape(kinds, slots, depth, EY)
    sides = jnp.stack([y_low, y_high], 0)
    padded = with_halo(sides, (("row", 0),), 1)
    same_front = front // slots == block
    same_back = back // slots == block
    ghost_front = gather_faces(y_high, front - base, (front >= 0) & same_front)
    ghost_front = ghost_front + gather_faces(
        padded[0], front % slots, (front >= 0) & jnp.logical_not(same_front)
    )
    ghost_back = gather_faces(y_low, back - base, (back >= 0) & same_back)
    ghost_back = ghost_back + gather_faces(
        padded[3], back % slots, (back >= 0) & jnp.logical_not(same_back)
    )
    spread_front = jnp.einsum(
        "ksdx,cx->ksdc",
        ghost_front.reshape(kinds, slots, depth, EX),
        pick_low,
        precision=lax.Precision.HIGHEST,
    )
    spread_back = jnp.einsum(
        "ksdx,cx->ksdc",
        ghost_back.reshape(kinds, slots, depth, EX),
        pick_high,
        precision=lax.Precision.HIGHEST,
    )
    position = jnp.arange(cells, dtype=jnp.int32) % EY
    blank = jnp.zeros((kinds, slots, depth, 1), jnp.float32)
    y_minus = jnp.where(position == 0, spread_front, jnp.concatenate([blank, field[..., :-1]], -1))
    y_plus = jnp.where(
        position == EY - 1, spread_back, jnp.concatenate([field[..., 1:], blank], -1)
    )
    x_minus = jnp.concatenate([ghost_left, field[..., : cells - EY]], -1)
    x_plus = jnp.concatenate([field[..., EY:], ghost_right], -1)
    z_minus = jnp.concatenate([below[:, :, None, :], field[:, :, :-1, :]], 2)
    z_plus = jnp.concatenate([field[:, :, 1:, :], above[:, :, None, :]], 2)
    return x_minus + x_plus + y_minus + y_plus + z_minus + z_plus


def advance(field, total, nsum, rate, rate_up, scaled):
    return (
        field + rate * (nsum - 6.0 * field) - rate_up * scaled[None] * field / (1.0 + total)[None]
    )


def per_device(ligand, density, counts, neighbours, diffusion, uptake):
    slots = ligand.shape[1]
    block = lax.axis_index(("cube", "row"))
    slot_ids = jnp.arange(slots, dtype=jnp.int32)
    filled = (slot_ids < counts[0])[None, :, None, None]
    field = jnp.where(filled, ligand, jnp.float32(0.0))
    scaled = density.astype(jnp.float32) / 8.0
    lower = neighbours[:, 4]
    upper = neighbours[:, 5]
    own = lax.axis_index("pair")
    rate = lax.dynamic_slice_in_dim(diffusion, own, 1, 0).reshape(1, 1, 1, 1)
    rate_up = lax.dynamic_slice_in_dim(uptake, own, 1, 0).reshape(1, 1, 1, 1)
    for step in range(STEPS):
        other = from_partner(field, "pair", 0)
        total = field[0] + other[0]
        z_faces = jnp.stack([field[:, :, 0, :], field[:, :, -1, :]], 0)
        stacked = with_halo(z_faces, (("cube", 0),), 1)
        below = gather_faces(stacked[0], lower % slots, lower >= 0)
        above = gather_faces(stacked[3], upper % slots, upper >= 0)
        nsum = neighbour_sum(field, below, above, neighbours, block)
        field = advance(field, total, nsum, rate, rate_up, scaled)
    return field


def solution(mesh):
    in_specs = (
        P("pair", ("groups", "cube", "row"), None, None),
        P(("groups", "cube", "row"), None, None),
        P(("groups", "cube", "row")),
        P(("groups", "cube", "row"), None),
        P(),
        P(),
    )
    out_specs = P("pair", ("groups", "cube", "row"), None, None)
    return jax.shard_map(
        per_device, mesh=mesh, in_specs=in_specs, out_specs=out_specs, check_vma=False
    )
```

profile of v0, /device:TPU:0, one launch (start us, length us, event | category | flops | bytes accessed | tf_op | source)
XLA Modules:
  0.0 93.7 jit_solution(4078591556024671053)
XLA Ops:
  0.7 1.2 %broadcast_select_fusion = f32[1,4,32,1024]{3,2,1,0:T(8,128)S(1)} fusion(f32[1,4,32,1024]{3,2,1,0:T(8,128)} %param.6, pred[4]{0:T(512)(128)(4,1)S(1)} %iota_compare_fusion.26), kind=kLoop, calls=%fused_computation.92 | loop fusion | flops 131072 | bytes 1048580 | tf_op jit(solution)/shard_map/jit(_where)/select_n | solution.py:115
  1.8 0.5 collective-permute-start.4
  2.4 4.5 %collective-permute-start.2 = (f32[1,1,4,1024]{3,0,2,1:T(1,128)S(1)}, f32[1,1,4,1024]{3,0,2,1:T(1,128)S(1)}, u32[]{:S(2)}, u32[]{:S(2)}) collective-permute-start(f32[1,1,4,1024]{3,0,2,1:T(1,128)S(1)} %get-tuple-element.57), channel_id=1, source_target_pairs={{0,4},{4,8},{8,12},{1,5},{5,9},{9,13},{2,6},{6,10},{10,14},{3,7},{... | collective-permute-start | bytes 49160 | tf_op jit(solution)/shard_map/ppermute | solution.py:19
  6.9 1.3 %collective-permute-start.3 = (f32[1,1,4,1024]{3,0,2,1:T(1,128)S(1)}, f32[1,1,4,1024]{3,0,2,1:T(1,128)S(1)}, u32[]{:S(2)}, u32[]{:S(2)}) collective-permute-start(f32[1,1,4,1024]{3,0,2,1:T(1,128)S(1)} %get-tuple-element.58), channel_id=1, source_target_pairs={{4,0},{8,4},{12,8},{5,1},{9,5},{13,9},{6,2},{10,6},{14,10},{7,3},{... | collective-permute-start | bytes 49160 | tf_op jit(solution)/shard_map/ppermute | solution.py:21
  8.2 0.6 fusion.55
  8.9 1.3 %collective-permute-start.1 = (f32[1,1,4,1024]{3,2,1,0:T(4,128)S(1)}, f32[1,1,4,1024]{3,2,1,0:T(4,128)S(1)}, u32[]{:S(2)}, u32[]{:S(2)}) collective-permute-start(f32[1,1,4,1024]{3,2,1,0:T(4,128)S(1)} %stack_reshape.25), channel_id=1, source_target_pairs={{2,0},{3,1},{6,4},{7,5},{10,8},{11,9},{14,12},{15,13},{18,16},{19,... | collective-permute-start | bytes 49160 | tf_op jit(solution)/shard_map/ppermute | solution.py:21
  10.2 0.6 fusion.57
  11.0 4.5 %collective-permute-start = (f32[1,1,4,1024]{3,2,1,0:T(4,128)S(1)}, f32[1,1,4,1024]{3,2,1,0:T(4,128)S(1)}, u32[]{:S(2)}, u32[]{:S(2)}) collective-permute-start(f32[1,1,4,1024]{3,2,1,0:T(4,128)S(1)} %stack_reshape.24), channel_id=1, source_target_pairs={{0,2},{1,3},{4,6},{5,7},{8,10},{9,11},{12,14},{13,15},{16,18},{17,... | collective-permute-start | bytes 49160 | tf_op jit(solution)/shard_map/ppermute | solution.py:19
  15.9 0.9 %fusion.406 = (f32[1,4,32,1023]{3,2,1,0:T(8,128)}, f32[1,4,32,1023]{3,2,1,0:T(8,128)S(1)}) fusion(f32[1,4,32,1024]{3,2,1,0:T(8,128)S(1)} %broadcast_select_fusion), kind=kLoop, calls=%fused_computation.505 | loop fusion | bytes 2095104 | tf_op jit(solution)/shard_map/slice | solution.py:93
  16.8 1.0 %fusion.408 = (f32[1,4,32,992]{3,2,1,0:T(8,128)S(1)}, f32[1,4,32,992]{3,2,1,0:T(8,128)}) fusion(f32[1,4,32,1024]{3,2,1,0:T(8,128)S(1)} %broadcast_select_fusion), kind=kLoop, calls=%fused_computation.507 | loop fusion | bytes 2031616 | tf_op jit(solution)/shard_map/slice | solution.py:97
  17.8 0.7 copy-done.7
  18.5 0.2 fusion.216
  18.7 0.3 subtract_reduce_fusion.3
  19.8 0.2 fusion.194
  20.6 0.6 copy-done.8
  21.3 0.6 dynamic_slice.7
  21.9 0.6 dynamic_slice.6
  24.3 0.6 fusion.8
  25.0 0.4 copy-done
  25.5 2.8 %fusion.48 = f32[1,4,32,1024]{3,2,1,0:T(8,128)S(1)} fusion(f32[1,4,32,1024]{3,2,1,0:T(8,128)S(1)} %broadcast_select_fusion, f32[1,4,32,1024]{3,2,1,0:T(8,128)} %collective-permute-done.4, f32[1,4,1,1024]{3,2,1,0:T(1,128)S(1)} %reshape_bitcast_fusion.6, f32[1,4,31,1024]{3,2,1,0:T(8,128)S(1)} %get-tuple-element.60, ...), kind=kOutput, calls=%fused_computation.80 | convolution fusion | flops 53149696 | bytes 5259912 | tf_op jit(solution)/shard_map/ksdx,cx->ksdc/dot_general | solution.py:79
  28.3 0.6 fusion.43
  29.1 0.6 fusion.45
  30.1 0.2 fusion.402
  30.3 0.2 fusion.404
  30.5 1.0 %fusion.403 = (f32[1,4,31,1024]{3,2,1,0:T(8,128)}, f32[1,4,31,1024]{3,2,1,0:T(8,128)}) fusion(f32[1,4,32,1024]{3,2,1,0:T(8,128)S(1)} %fusion.48), kind=kLoop, calls=%fused_computation.502 | loop fusion | bytes 2031616 | tf_op jit(solution)/shard_map/slice | solution.py:100
  31.5 1.3 %collective-permute-start.8 = (f32[1,1,4,1024]{3,0,2,1:T(1,128)S(1)}, f32[1,1,4,1024]{3,0,2,1:T(1,128)S(1)}, u32[]{:S(2)}, u32[]{:S(2)}) collective-permute-start(f32[1,1,4,1024]{3,0,2,1:T(1,128)S(1)} %get-tuple-element.45), channel_id=1, source_target_pairs={{4,0},{8,4},{12,8},{5,1},{9,5},{13,9},{6,2},{10,6},{14,10},{7,3},{... | collective-permute-start | bytes 49160 | tf_op jit(solution)/shard_map/ppermute | solution.py:21
  32.8 5.2 %collective-permute-start.7 = (f32[1,1,4,1024]{3,0,2,1:T(1,128)S(1)}, f32[1,1,4,1024]{3,0,2,1:T(1,128)S(1)}, u32[]{:S(2)}, u32[]{:S(2)}) collective-permute-start(f32[1,1,4,1024]{3,0,2,1:T(1,128)S(1)} %get-tuple-element.46), channel_id=1, source_target_pairs={{0,4},{4,8},{8,12},{1,5},{5,9},{9,13},{2,6},{6,10},{10,14},{3,7},{... | collective-permute-start | bytes 49160 | tf_op jit(solution)/shard_map/ppermute | solution.py:19
  38.2 1.3 %collective-permute-start.6 = (f32[1,1,4,1024]{3,2,1,0:T(4,128)S(1)}, f32[1,1,4,1024]{3,2,1,0:T(4,128)S(1)}, u32[]{:S(2)}, u32[]{:S(2)}) collective-permute-start(f32[1,1,4,1024]{3,2,1,0:T(4,128)S(1)} %stack_reshape.27), channel_id=1, source_target_pairs={{2,0},{3,1},{6,4},{7,5},{10,8},{11,9},{14,12},{15,13},{18,16},{19,... | collective-permute-start | bytes 49160 | tf_op jit(solution)/shard_map/ppermute | solution.py:21
  39.6 4.5 %collective-permute-start.5 = (f32[1,1,4,1024]{3,2,1,0:T(4,128)S(1)}, f32[1,1,4,1024]{3,2,1,0:T(4,128)S(1)}, u32[]{:S(2)}, u32[]{:S(2)}) collective-permute-start(f32[1,1,4,1024]{3,2,1,0:T(4,128)S(1)} %stack_reshape.26), channel_id=1, source_target_pairs={{0,2},{1,3},{4,6},{5,7},{8,10},{9,11},{12,14},{13,15},{16,18},{17,... | collective-permute-start | bytes 49160 | tf_op jit(solution)/shard_map/ppermute | solution.py:19
  44.3 0.2 convolution_bitcast_fusion.12
  44.6 0.2 convolution_bitcast_fusion.13
  45.5 0.2 collective-permute-done.5
  46.0 0.6 fusion.14
  46.6 0.4 copy-done.3
  47.2 0.8 fusion.13
  48.0 1.9 %fusion.50 = f32[1,4,32,1024]{3,2,1,0:T(8,128)S(1)} fusion(f32[1,4,32,1024]{3,2,1,0:T(8,128)S(1)} %fusion.48, f32[1,4,32,1024]{3,2,1,0:T(8,128)} %collective-permute-done.9, f32[1,4,32,1024]{3,2,1,0:T(8,128)S(1)} %fusion.13, s32[4,32,1024]{2,1,0:T(8,128)S(1)} %copy-done, f32[]{:T(128)} %bitcast.23, f32[]{:T(128)} %bitcast.1), kind=kLoop, calls=%fused_computation.82 | loop fusion | flops 1441792 | bytes 2621448 | tf_op jit(solution)/shard_map/sub | solution.py:106
  49.9 0.6 fusion.39
  50.7 0.6 fusion.41
  51.7 1.0 %fusion.398 = (f32[1,4,32,1023]{3,2,1,0:T(8,128)S(1)}, f32[1,4,32,1023]{3,2,1,0:T(8,128)}) fusion(f32[1,4,32,1024]{3,2,1,0:T(8,128)S(1)} %fusion.50), kind=kLoop, calls=%fused_computation.497 | loop fusion | bytes 2095104 | tf_op jit(solution)/shard_map/slice | solution.py:93
  52.7 0.2 fusion.400
  52.9 0.9 fusion.399
  53.7 1.3 %collective-permute-start.13 = (f32[1,1,4,1024]{3,0,2,1:T(1,128)S(1)}, f32[1,1,4,1024]{3,0,2,1:T(1,128)S(1)}, u32[]{:S(2)}, u32[]{:S(2)}) collective-permute-start(f32[1,1,4,1024]{3,0,2,1:T(1,128)S(1)} %get-tuple-element.35), channel_id=1, source_target_pairs={{4,0},{8,4},{12,8},{5,1},{9,5},{13,9},{6,2},{10,6},{14,10},{7,3},{... | collective-permute-start | bytes 49160 | tf_op jit(solution)/shard_map/ppermute | solution.py:21
  55.0 4.6 %collective-permute-start.12 = (f32[1,1,4,1024]{3,0,2,1:T(1,128)S(1)}, f32[1,1,4,1024]{3,0,2,1:T(1,128)S(1)}, u32[]{:S(2)}, u32[]{:S(2)}) collective-permute-start(f32[1,1,4,1024]{3,0,2,1:T(1,128)S(1)} %get-tuple-element.36), channel_id=1, source_target_pairs={{0,4},{4,8},{8,12},{1,5},{5,9},{9,13},{2,6},{6,10},{10,14},{3,7},{... | collective-permute-start | bytes 49160 | tf_op jit(solution)/shard_map/ppermute | solution.py:19
  59.8 1.3 %collective-permute-start.11 = (f32[1,1,4,1024]{3,2,1,0:T(4,128)S(1)}, f32[1,1,4,1024]{3,2,1,0:T(4,128)S(1)}, u32[]{:S(2)}, u32[]{:S(2)}) collective-permute-start(f32[1,1,4,1024]{3,2,1,0:T(4,128)S(1)} %stack_reshape.29), channel_id=1, source_target_pairs={{2,0},{3,1},{6,4},{7,5},{10,8},{11,9},{14,12},{15,13},{18,16},{19,... | collective-permute-start | bytes 49160 | tf_op jit(solution)/shard_map/ppermute | solution.py:21
  61.2 4.7 %collective-permute-start.10 = (f32[1,1,4,1024]{3,2,1,0:T(4,128)S(1)}, f32[1,1,4,1024]{3,2,1,0:T(4,128)S(1)}, u32[]{:S(2)}, u32[]{:S(2)}) collective-permute-start(f32[1,1,4,1024]{3,2,1,0:T(4,128)S(1)} %stack_reshape.28), channel_id=1, source_target_pairs={{0,2},{1,3},{4,6},{5,7},{8,10},{9,11},{12,14},{13,15},{16,18},{17,... | collective-permute-start | bytes 49160 | tf_op jit(solution)/shard_map/ppermute | solution.py:19
  66.1 0.2 convolution_bitcast_fusion.10
  66.3 0.2 convolution_bitcast_fusion.11
  67.6 1.7 %fusion.20 = f32[1,4,32,1024]{3,2,1,0:T(8,128)S(1)} fusion(f32[4,32,32]{2,1,0:T(8,128)S(1)} %reshape.576, f32[1,4,32,1023]{3,2,1,0:T(8,128)} %get-tuple-element.32, pred[1024]{0:T(1024)(128)(4,1)S(1)} %fusion.173, s32[32]{0:T(128)S(1)} %broadcast_add_fusion), kind=kOutput, calls=%fused_computation.28 | convolution fusion | flops 50528256 | bytes 1065600 | tf_op jit(solution)/shard_map/ksdx,cx->ksdc/dot_general | solution.py:85
  69.3 0.8 fusion.19
  70.1 1.9 %fusion.52 = f32[1,4,32,1024]{3,2,1,0:T(8,128)S(1)} fusion(f32[1,4,32,1024]{3,2,1,0:T(8,128)S(1)} %fusion.50, f32[1,4,32,1024]{3,2,1,0:T(8,128)} %collective-permute-done.14, f32[1,4,32,1024]{3,2,1,0:T(8,128)S(1)} %fusion.19, s32[4,32,1024]{2,1,0:T(8,128)S(1)} %copy-done, f32[]{:T(128)} %bitcast.23, f32[]{:T(128)} %bitcast.1), kind=kLoop, calls=%fused_computation.84 | loop fusion | flops 1441792 | bytes 2621448 | tf_op jit(solution)/shard_map/sub | solution.py:106
  72.0 0.6 fusion.35
  72.8 0.6 fusion.37
  73.8 0.2 fusion.394
  74.0 0.2 fusion.396
  74.2 1.0 %fusion.395 = (f32[1,4,31,1024]{3,2,1,0:T(8,128)}, f32[1,4,31,1024]{3,2,1,0:T(8,128)}) fusion(f32[1,4,32,1024]{3,2,1,0:T(8,128)S(1)} %fusion.52), kind=kLoop, calls=%fused_computation.494 | loop fusion | bytes 2031616 | tf_op jit(solution)/shard_map/slice | solution.py:100
  75.3 1.3 %collective-permute-start.18 = (f32[1,1,4,1024]{3,0,2,1:T(1,128)S(1)}, f32[1,1,4,1024]{3,0,2,1:T(1,128)S(1)}, u32[]{:S(2)}, u32[]{:S(2)}) collective-permute-start(f32[1,1,4,1024]{3,0,2,1:T(1,128)S(1)} %get-tuple-element.25), channel_id=1, source_target_pairs={{4,0},{8,4},{12,8},{5,1},{9,5},{13,9},{6,2},{10,6},{14,10},{7,3},{... | collective-permute-start | bytes 49160 | tf_op jit(solution)/shard_map/ppermute | solution.py:21
  76.5 4.5 %collective-permute-start.17 = (f32[1,1,4,1024]{3,0,2,1:T(1,128)S(1)}, f32[1,1,4,1024]{3,0,2,1:T(1,128)S(1)}, u32[]{:S(2)}, u32[]{:S(2)}) collective-permute-start(f32[1,1,4,1024]{3,0,2,1:T(1,128)S(1)} %get-tuple-element.26), channel_id=1, source_target_pairs={{0,4},{4,8},{8,12},{1,5},{5,9},{9,13},{2,6},{6,10},{10,14},{3,7},{... | collective-permute-start | bytes 49160 | tf_op jit(solution)/shard_map/ppermute | solution.py:19
  81.3 1.3 %collective-permute-start.16 = (f32[1,1,4,1024]{3,2,1,0:T(4,128)S(1)}, f32[1,1,4,1024]{3,2,1,0:T(4,128)S(1)}, u32[]{:S(2)}, u32[]{:S(2)}) collective-permute-start(f32[1,1,4,1024]{3,2,1,0:T(4,128)S(1)} %stack_reshape.31), channel_id=1, source_target_pairs={{2,0},{3,1},{6,4},{7,5},{10,8},{11,9},{14,12},{15,13},{18,16},{19,... | collective-permute-start | bytes 49160 | tf_op jit(solution)/shard_map/ppermute | solution.py:21
  82.7 4.5 %collective-permute-start.15 = (f32[1,1,4,1024]{3,2,1,0:T(4,128)S(1)}, f32[1,1,4,1024]{3,2,1,0:T(4,128)S(1)}, u32[]{:S(2)}, u32[]{:S(2)}) collective-permute-start(f32[1,1,4,1024]{3,2,1,0:T(4,128)S(1)} %stack_reshape.30), channel_id=1, source_target_pairs={{0,2},{1,3},{4,6},{5,7},{8,10},{9,11},{12,14},{13,15},{16,18},{17,... | collective-permute-start | bytes 49160 | tf_op jit(solution)/shard_map/ppermute | solution.py:19
  88.5 0.2 collective-permute-done.15
  89.1 0.6 fusion.26
  89.7 0.4 copy-done.1
  90.3 0.8 fusion.25
  91.1 2.7 %fusion.54 = f32[1,4,32,1024]{3,2,1,0:T(8,128)} fusion(f32[1,4,32,1024]{3,2,1,0:T(8,128)S(1)} %fusion.52, f32[1,4,32,1024]{3,2,1,0:T(8,128)} %collective-permute-done.19, f32[1,4,32,1024]{3,2,1,0:T(8,128)S(1)} %fusion.25, s32[4,32,1024]{2,1,0:T(8,128)S(1)} %copy-done, f32[]{:T(128)} %bitcast.23, f32[]{:T(128)} %bitcast.1), kind=kLoop, calls=%fused_computation.86 | loop fusion | flops 1441792 | bytes 2621448 | tf_op jit(solution)/shard_map/sub | solution.py:106
  (132 shorter events, 10.1 us)
Async XLA Ops:
  1.8 23.1 %collective-permute-start.4 = (f32[1,4,32,1024]{3,2,1,0:T(8,128)S(1)}, f32[1,4,32,1024]{3,2,1,0:T(8,128)}, u32[]{:S(2)}, u32[]{:S(2)}) collective-permute-start(f32[1,4,32,1024]{3,2,1,0:T(8,128)S(1)} %broadcast_select_fusion), channel_id=1, source_target_pairs={{0,1},{1,0},{2,3},{3,2},{4,5},{5,4},{6,7},{7,6},{8,9},{9,8},{10,11... | collective-permute-start | bytes 1572872 | tf_op jit(solution)/shard_map/ppermute | solution.py:31
  2.4 21.0 %collective-permute-start.2 = (f32[1,1,4,1024]{3,0,2,1:T(1,128)S(1)}, f32[1,1,4,1024]{3,0,2,1:T(1,128)S(1)}, u32[]{:S(2)}, u32[]{:S(2)}) collective-permute-start(f32[1,1,4,1024]{3,0,2,1:T(1,128)S(1)} %get-tuple-element.57), channel_id=1, source_target_pairs={{0,4},{4,8},{8,12},{1,5},{5,9},{9,13},{2,6},{6,10},{10,14},{3,7},{... | collective-permute-start | bytes 49160 | tf_op jit(solution)/shard_map/ppermute | solution.py:19
  6.9 17.2 %collective-permute-start.3 = (f32[1,1,4,1024]{3,0,2,1:T(1,128)S(1)}, f32[1,1,4,1024]{3,0,2,1:T(1,128)S(1)}, u32[]{:S(2)}, u32[]{:S(2)}) collective-permute-start(f32[1,1,4,1024]{3,0,2,1:T(1,128)S(1)} %get-tuple-element.58), channel_id=1, source_target_pairs={{4,0},{8,4},{12,8},{5,1},{9,5},{13,9},{6,2},{10,6},{14,10},{7,3},{... | collective-permute-start | bytes 49160 | tf_op jit(solution)/shard_map/ppermute | solution.py:21
  8.9 14.6 %collective-permute-start.1 = (f32[1,1,4,1024]{3,2,1,0:T(4,128)S(1)}, f32[1,1,4,1024]{3,2,1,0:T(4,128)S(1)}, u32[]{:S(2)}, u32[]{:S(2)}) collective-permute-start(f32[1,1,4,1024]{3,2,1,0:T(4,128)S(1)} %stack_reshape.25), channel_id=1, source_target_pairs={{2,0},{3,1},{6,4},{7,5},{10,8},{11,9},{14,12},{15,13},{18,16},{19,... | collective-permute-start | bytes 49160 | tf_op jit(solution)/shard_map/ppermute | solution.py:21
  11.0 12.8 %collective-permute-start = (f32[1,1,4,1024]{3,2,1,0:T(4,128)S(1)}, f32[1,1,4,1024]{3,2,1,0:T(4,128)S(1)}, u32[]{:S(2)}, u32[]{:S(2)}) collective-permute-start(f32[1,1,4,1024]{3,2,1,0:T(4,128)S(1)} %stack_reshape.24), channel_id=1, source_target_pairs={{0,2},{1,3},{4,6},{5,7},{8,10},{9,11},{12,14},{13,15},{16,18},{17,... | collective-permute-start | bytes 49160 | tf_op jit(solution)/shard_map/ppermute | solution.py:19
  17.8 0.7 copy-start.7
  20.6 0.7 copy-start.8
  21.3 0.7 copy-start.9
  24.3 1.0 %copy-start = (s32[4,32,1024]{2,1,0:T(8,128)S(1)}, s32[4,32,1024]{2,1,0:T(8,128)}, u32[]{:S(2)}) copy-start(s32[4,32,1024]{2,1,0:T(8,128)} %param.7) | copy-start | bytes 1572868
  24.3 1.2 %copy-start.6 = (f32[1,4,32,1023]{3,2,1,0:T(8,128)S(1)}, f32[1,4,32,1023]{3,2,1,0:T(8,128)}, u32[]{:S(2)}) copy-start(f32[1,4,32,1023]{3,2,1,0:T(8,128)} %get-tuple-element.51) | copy-start | bytes 1571332
  30.0 17.9 %collective-permute-start.9 = (f32[1,4,32,1024]{3,2,1,0:T(8,128)S(1)}, f32[1,4,32,1024]{3,2,1,0:T(8,128)}, u32[]{:S(2)}, u32[]{:S(2)}) collective-permute-start(f32[1,4,32,1024]{3,2,1,0:T(8,128)S(1)} %fusion.48), channel_id=1, source_target_pairs={{0,1},{1,0},{2,3},{3,2},{4,5},{5,4},{6,7},{7,6},{8,9},{9,8},{10,11... | collective-permute-start | bytes 1572872 | tf_op jit(solution)/shard_map/ppermute | solution.py:31
  31.5 13.4 %collective-permute-start.8 = (f32[1,1,4,1024]{3,0,2,1:T(1,128)S(1)}, f32[1,1,4,1024]{3,0,2,1:T(1,128)S(1)}, u32[]{:S(2)}, u32[]{:S(2)}) collective-permute-start(f32[1,1,4,1024]{3,0,2,1:T(1,128)S(1)} %get-tuple-element.45), channel_id=1, source_target_pairs={{4,0},{8,4},{12,8},{5,1},{9,5},{13,9},{6,2},{10,6},{14,10},{7,3},{... | collective-permute-start | bytes 49160 | tf_op jit(solution)/shard_map/ppermute | solution.py:21
  32.8 12.3 %collective-permute-start.7 = (f32[1,1,4,1024]{3,0,2,1:T(1,128)S(1)}, f32[1,1,4,1024]{3,0,2,1:T(1,128)S(1)}, u32[]{:S(2)}, u32[]{:S(2)}) collective-permute-start(f32[1,1,4,1024]{3,0,2,1:T(1,128)S(1)} %get-tuple-element.46), channel_id=1, source_target_pairs={{0,4},{4,8},{8,12},{1,5},{5,9},{9,13},{2,6},{6,10},{10,14},{3,7},{... | collective-permute-start | bytes 49160 | tf_op jit(solution)/shard_map/ppermute | solution.py:19
  38.2 7.1 %collective-permute-start.6 = (f32[1,1,4,1024]{3,2,1,0:T(4,128)S(1)}, f32[1,1,4,1024]{3,2,1,0:T(4,128)S(1)}, u32[]{:S(2)}, u32[]{:S(2)}) collective-permute-start(f32[1,1,4,1024]{3,2,1,0:T(4,128)S(1)} %stack_reshape.27), channel_id=1, source_target_pairs={{2,0},{3,1},{6,4},{7,5},{10,8},{11,9},{14,12},{15,13},{18,16},{19,... | collective-permute-start | bytes 49160 | tf_op jit(solution)/shard_map/ppermute | solution.py:21
  39.6 6.0 %collective-permute-start.5 = (f32[1,1,4,1024]{3,2,1,0:T(4,128)S(1)}, f32[1,1,4,1024]{3,2,1,0:T(4,128)S(1)}, u32[]{:S(2)}, u32[]{:S(2)}) collective-permute-start(f32[1,1,4,1024]{3,2,1,0:T(4,128)S(1)} %stack_reshape.26), channel_id=1, source_target_pairs={{0,2},{1,3},{4,6},{5,7},{8,10},{9,11},{12,14},{13,15},{16,18},{17,... | collective-permute-start | bytes 49160 | tf_op jit(solution)/shard_map/ppermute | solution.py:19
  46.0 1.0 %copy-start.3 = (f32[1,4,31,1024]{3,2,1,0:T(8,128)S(1)}, f32[1,4,31,1024]{3,2,1,0:T(8,128)}, u32[]{:S(2)}) copy-start(f32[1,4,31,1024]{3,2,1,0:T(8,128)} %get-tuple-element.43) | copy-start | bytes 1523716
  46.0 1.2 %copy-start.4 = (f32[1,4,31,1024]{3,2,1,0:T(8,128)S(1)}, f32[1,4,31,1024]{3,2,1,0:T(8,128)}, u32[]{:S(2)}) copy-start(f32[1,4,31,1024]{3,2,1,0:T(8,128)} %get-tuple-element.44) | copy-start | bytes 1523716
  51.6 18.5 %collective-permute-start.14 = (f32[1,4,32,1024]{3,2,1,0:T(8,128)S(1)}, f32[1,4,32,1024]{3,2,1,0:T(8,128)}, u32[]{:S(2)}, u32[]{:S(2)}) collective-permute-start(f32[1,4,32,1024]{3,2,1,0:T(8,128)S(1)} %fusion.50), channel_id=1, source_target_pairs={{0,1},{1,0},{2,3},{3,2},{4,5},{5,4},{6,7},{7,6},{8,9},{9,8},{10,11... | collective-permute-start | bytes 1572872 | tf_op jit(solution)/shard_map/ppermute | solution.py:31
  53.7 12.9 %collective-permute-start.13 = (f32[1,1,4,1024]{3,0,2,1:T(1,128)S(1)}, f32[1,1,4,1024]{3,0,2,1:T(1,128)S(1)}, u32[]{:S(2)}, u32[]{:S(2)}) collective-permute-start(f32[1,1,4,1024]{3,0,2,1:T(1,128)S(1)} %get-tuple-element.35), channel_id=1, source_target_pairs={{4,0},{8,4},{12,8},{5,1},{9,5},{13,9},{6,2},{10,6},{14,10},{7,3},{... | collective-permute-start | bytes 49160 | tf_op jit(solution)/shard_map/ppermute | solution.py:21
  55.0 11.8 %collective-permute-start.12 = (f32[1,1,4,1024]{3,0,2,1:T(1,128)S(1)}, f32[1,1,4,1024]{3,0,2,1:T(1,128)S(1)}, u32[]{:S(2)}, u32[]{:S(2)}) collective-permute-start(f32[1,1,4,1024]{3,0,2,1:T(1,128)S(1)} %get-tuple-element.36), channel_id=1, source_target_pairs={{0,4},{4,8},{8,12},{1,5},{5,9},{9,13},{2,6},{6,10},{10,14},{3,7},{... | collective-permute-start | bytes 49160 | tf_op jit(solution)/shard_map/ppermute | solution.py:19
  59.8 7.3 %collective-permute-start.11 = (f32[1,1,4,1024]{3,2,1,0:T(4,128)S(1)}, f32[1,1,4,1024]{3,2,1,0:T(4,128)S(1)}, u32[]{:S(2)}, u32[]{:S(2)}) collective-permute-start(f32[1,1,4,1024]{3,2,1,0:T(4,128)S(1)} %stack_reshape.29), channel_id=1, source_target_pairs={{2,0},{3,1},{6,4},{7,5},{10,8},{11,9},{14,12},{15,13},{18,16},{19,... | collective-permute-start | bytes 49160 | tf_op jit(solution)/shard_map/ppermute | solution.py:21
  61.2 6.0 %collective-permute-start.10 = (f32[1,1,4,1024]{3,2,1,0:T(4,128)S(1)}, f32[1,1,4,1024]{3,2,1,0:T(4,128)S(1)}, u32[]{:S(2)}, u32[]{:S(2)}) collective-permute-start(f32[1,1,4,1024]{3,2,1,0:T(4,128)S(1)} %stack_reshape.28), channel_id=1, source_target_pairs={{0,2},{1,3},{4,6},{5,7},{8,10},{9,11},{12,14},{13,15},{16,18},{17,... | collective-permute-start | bytes 49160 | tf_op jit(solution)/shard_map/ppermute | solution.py:19
  67.6 1.7 %copy-start.5 = (f32[1,4,31,1024]{3,2,1,0:T(8,128)S(1)}, f32[1,4,31,1024]{3,2,1,0:T(8,128)}, u32[]{:S(2)}) copy-start(f32[1,4,31,1024]{3,2,1,0:T(8,128)} %get-tuple-element.34) | copy-start | bytes 1523716
  73.7 17.3 %collective-permute-start.19 = (f32[1,4,32,1024]{3,2,1,0:T(8,128)S(1)}, f32[1,4,32,1024]{3,2,1,0:T(8,128)}, u32[]{:S(2)}, u32[]{:S(2)}) collective-permute-start(f32[1,4,32,1024]{3,2,1,0:T(8,128)S(1)} %fusion.52), channel_id=1, source_target_pairs={{0,1},{1,0},{2,3},{3,2},{4,5},{5,4},{6,7},{7,6},{8,9},{9,8},{10,11... | collective-permute-start | bytes 1572872 | tf_op jit(solution)/shard_map/ppermute | solution.py:31
  75.3 12.7 %collective-permute-start.18 = (f32[1,1,4,1024]{3,0,2,1:T(1,128)S(1)}, f32[1,1,4,1024]{3,0,2,1:T(1,128)S(1)}, u32[]{:S(2)}, u32[]{:S(2)}) collective-permute-start(f32[1,1,4,1024]{3,0,2,1:T(1,128)S(1)} %get-tuple-element.25), channel_id=1, source_target_pairs={{4,0},{8,4},{12,8},{5,1},{9,5},{13,9},{6,2},{10,6},{14,10},{7,3},{... | collective-permute-start | bytes 49160 | tf_op jit(solution)/shard_map/ppermute | solution.py:21
  76.5 11.6 %collective-permute-start.17 = (f32[1,1,4,1024]{3,0,2,1:T(1,128)S(1)}, f32[1,1,4,1024]{3,0,2,1:T(1,128)S(1)}, u32[]{:S(2)}, u32[]{:S(2)}) collective-permute-start(f32[1,1,4,1024]{3,0,2,1:T(1,128)S(1)} %get-tuple-element.26), channel_id=1, source_target_pairs={{0,4},{4,8},{8,12},{1,5},{5,9},{9,13},{2,6},{6,10},{10,14},{3,7},{... | collective-permute-start | bytes 49160 | tf_op jit(solution)/shard_map/ppermute | solution.py:19
  81.3 7.1 %collective-permute-start.16 = (f32[1,1,4,1024]{3,2,1,0:T(4,128)S(1)}, f32[1,1,4,1024]{3,2,1,0:T(4,128)S(1)}, u32[]{:S(2)}, u32[]{:S(2)}) collective-permute-start(f32[1,1,4,1024]{3,2,1,0:T(4,128)S(1)} %stack_reshape.31), channel_id=1, source_target_pairs={{2,0},{3,1},{6,4},{7,5},{10,8},{11,9},{14,12},{15,13},{18,16},{19,... | collective-permute-start | bytes 49160 | tf_op jit(solution)/shard_map/ppermute | solution.py:21
  82.7 6.0 %collective-permute-start.15 = (f32[1,1,4,1024]{3,2,1,0:T(4,128)S(1)}, f32[1,1,4,1024]{3,2,1,0:T(4,128)S(1)}, u32[]{:S(2)}, u32[]{:S(2)}) collective-permute-start(f32[1,1,4,1024]{3,2,1,0:T(4,128)S(1)} %stack_reshape.30), channel_id=1, source_target_pairs={{0,2},{1,3},{4,6},{5,7},{8,10},{9,11},{12,14},{13,15},{16,18},{17,... | collective-permute-start | bytes 49160 | tf_op jit(solution)/shard_map/ppermute | solution.py:19
  89.1 1.0 %copy-start.1 = (f32[1,4,31,1024]{3,2,1,0:T(8,128)S(1)}, f32[1,4,31,1024]{3,2,1,0:T(8,128)}, u32[]{:S(2)}) copy-start(f32[1,4,31,1024]{3,2,1,0:T(8,128)} %get-tuple-element.23) | copy-start | bytes 1523716
  89.1 1.2 %copy-start.2 = (f32[1,4,31,1024]{3,2,1,0:T(8,128)S(1)}, f32[1,4,31,1024]{3,2,1,0:T(8,128)}, u32[]{:S(2)}) copy-start(f32[1,4,31,1024]{3,2,1,0:T(8,128)} %get-tuple-element.24) | copy-start | bytes 1523716
where the time goes:
time: 94.6 us; the launch traced here: 93.7 us
  starting transfers between devices  48.1 us (51%)
  matrix products  18.8 us (20%)
  local copies, waits for them, and re-layouts  15.5 us (16%)
  other arithmetic  8.82 us (9%)
  between operations  2.16 us (2%)
    ppermute x8, starting transfers between devices, with_halo(): lax.ppermute(tail, axis, [(i, (i + 1) % count) for i in range(ends)])  37.1 us
    ppermute x8, starting transfers between devices, with_halo(): lax.ppermute(head, axis, [((i + 1) % count, i) for i in range(ends)])  10.3 us
    sub x3, other arithmetic, advance(): field + rate * (nsum - 6.0 * field)  6.42 us
    dot_general x32, matrix products, gather_faces(): jnp.einsum('ts,ksf->ktf', select, faces, precision=lax.Precision.HIGHEST)  5.17 us
    dot_general x4, matrix products, neighbour_sum(): jnp.einsum('ksdx,cx->ksdc', ghost_front.reshape(kinds, slots, depth, EX),...  5.04 us
    dot_general x4, matrix products, neighbour_sum(): jnp.einsum('ksdx,cx->ksdc', ghost_back.reshape(kinds, slots, depth, EX),...  3.55 us
    unnamed x20, local copies, waits for them, and re-layouts  3.1 us
    slice x3, local copies, waits for them, and re-layouts, neighbour_sum(): z_plus = jnp.concatenate([field[:, :, 1:, :], above[:, :, None, :]], 2)  2.95 us
  transfers between devices with their start and end apart: 20, of which 2 were waited for; matrix products, arithmetic and copies ran while one was open for 26% of the time, Pallas kernels for 0%

commit v1 on v0

v1 whole, which is shorter than its diff:
```python
import functools

import jax
import jax.numpy as jnp
from jax import lax
from jax.experimental import pallas as pl
from jax.experimental.pallas import tpu as pltpu
from jax.sharding import PartitionSpec as P

EY = 32
STEPS = 4
LANES = 128
ROWS = 8
MESH = pl.DeviceIdType.MESH


def kernel(
    layers, bands, slots, half, cells,
    nbr, counts, diffusion, uptake, ligand, density, out,
    field, dens, stage, y_own, y_minus, y_plus, z_low, z_high, z_minus, z_plus,
    load_sem, swap_send, swap_recv, face_send, face_recv, out_send, out_recv,
):
    core = lax.axis_index("pair")
    layer = lax.axis_index("cube")
    band = lax.axis_index("row")
    block = layer * bands + band
    other = 1 - core
    columns = cells // LANES
    has_minus = band > 0
    has_plus = band < bands - 1
    far_layer = jnp.where(core == 0, layer - 1, layer + 1)
    has_far = jnp.logical_and(far_layer >= 0, far_layer < layers)
    partner_id = {"pair": other}
    far_id = {"cube": far_layer, "pair": other}
    minus_id = {"row": band - 1}
    plus_id = {"row": band + 1}

    own_rows = pl.ds(pl.multiple_of(core * half, half), half)
    other_rows = pl.ds(pl.multiple_of(other * half, half), half)
    loads = [
        pltpu.make_async_copy(ligand.at[0, :, own_rows, :], field.at[0, core], load_sem.at[0]),
        pltpu.make_async_copy(density.at[:, own_rows, :], dens, load_sem.at[1]),
    ]
    for load in loads:
        load.start()

    barrier = pltpu.get_barrier_semaphore()
    pl.semaphore_signal(barrier, inc=1, device_id=partner_id, device_id_type=MESH)

    @pl.when(has_far)
    def _():
        pl.semaphore_signal(barrier, inc=1, device_id=far_id, device_id_type=MESH)

    @pl.when(has_minus)
    def _():
        pl.semaphore_signal(barrier, inc=1, device_id=minus_id, device_id_type=MESH)

    @pl.when(has_plus)
    def _():
        pl.semaphore_signal(barrier, inc=1, device_id=plus_id, device_id_type=MESH)

    peers = 1 + has_far.astype(jnp.int32) + has_minus.astype(jnp.int32) + has_plus.astype(jnp.int32)
    pl.semaphore_wait(barrier, peers)

    swap = pltpu.make_async_remote_copy(
        src_ref=ligand.at[0, :, other_rows, :], dst_ref=field.at[0, core],
        send_sem=swap_send, recv_sem=swap_recv, device_id=partner_id, device_id_type=MESH,
    )
    swap_in = pltpu.make_async_remote_copy(
        src_ref=ligand.at[0, :, other_rows, :], dst_ref=field.at[0, other],
        send_sem=swap_send, recv_sem=swap_recv, device_id=partner_id, device_id_type=MESH,
    )
    swap.start()

    def remote(source, target, step, k, device):
        return pltpu.make_async_remote_copy(
            src_ref=source.at[step], dst_ref=target[step],
            send_sem=face_send.at[step, k], recv_sem=face_recv.at[step, k],
            device_id=device, device_id_type=MESH,
        )

    def messages(step):
        first, last = core == 0, core == 1
        up_far = remote(z_high, z_minus, step, 0, far_id)
        up_near = remote(z_high, z_minus, step, 0, partner_id)
        down_far = remote(z_low, z_plus, step, 1, far_id)
        down_near = remote(z_low, z_plus, step, 1, partner_id)
        to_plus = remote(y_own, y_minus, step, 2, plus_id)
        to_minus = remote(y_own, y_plus, step, 3, minus_id)
        both = jnp.logical_and
        sends = [
            (both(last, has_far), up_far), (first, up_near),
            (both(first, has_far), down_far), (last, down_near),
            (has_plus, to_plus), (has_minus, to_minus),
        ]
        receives = [
            (jnp.logical_or(last, has_far), up_near), (jnp.logical_or(first, has_far), down_near),
            (has_minus, to_plus), (has_plus, to_minus),
        ]
        return sends, receives

    def send_faces(step):
        for wanted, copy in messages(step)[0]:
            pl.when(wanted)(copy.start)

    def wait_faces(step):
        for wanted, copy in messages(step)[1]:
            pl.when(wanted)(copy.wait_recv)

    def wait_sent(step):
        for wanted, copy in messages(step)[0]:
            pl.when(wanted)(copy.wait_send)

    lane = lax.broadcasted_iota(jnp.int32, (ROWS, LANES), 1)
    pair_of = lax.rem(lane + 1, EY) // 2
    even = lax.rem(lane, 2) == 0
    wide = lax.broadcasted_iota(jnp.int32, (half, LANES), 1)
    at_low = lax.rem(wide, EY) == 0
    at_high = lax.rem(wide, EY) == EY - 1
    below_32 = wide < EY
    above_96 = wide >= LANES - EY

    def roll(value, shift):
        shift = shift % LANES
        return value if shift == 0 else pltpu.roll(value, shift, axis=1)

    pieces = [(zv, j) for zv in range(half // ROWS) for j in range(columns)]

    def put_faces(step, species, tile, parts):
        packed = None
        for m, (zv, j) in enumerate(pieces):
            piece = roll(parts[j][zv * ROWS : (zv + 1) * ROWS], 2 * m)
            packed = piece if packed is None else jnp.where(pair_of == m, piece, packed)
        y_own[step, species, tile] = packed
        for j in range(columns):
            at = slice(j * LANES, (j + 1) * LANES)
            z_low[step, species, tile, :, at] = parts[j][:1]
            z_high[step, species, tile, :, at] = parts[j][half - 1 :]

    def columns_of(value):
        return [value[:, j * LANES : (j + 1) * LANES] for j in range(columns)]

    def first_faces(tile, carry):
        for species in range(2):
            put_faces(0, species, tile, columns_of(field[0, species, tile]))
        return carry

    zero = jnp.float32(0.0)

    def advance(step, tile):
        now, later = step % 2, (step + 1) % 2
        filled = tile < counts[0]

        def entry(k):
            value = nbr[tile, k]
            safe = jnp.maximum(value, 0)
            return value >= 0, lax.rem(safe, slots), safe // slots == block

        left_ok, left, _ = entry(0)
        right_ok, right, _ = entry(1)
        front_ok, front, front_here = entry(2)
        back_ok, back, back_here = entry(3)
        lower_ok, lower, _ = entry(4)
        upper_ok, upper, _ = entry(5)
        first = core == 0
        lower = jnp.where(first, lower, tile)
        lower_ok = jnp.where(first, lower_ok, filled)
        upper = jnp.where(first, tile, upper)
        upper_ok = jnp.where(first, filled, upper_ok)

        fields, sums = [], []
        for species in range(2):
            parts = columns_of(field[now, species, tile])
            if step == 0:
                parts = [jnp.where(filled, part, zero) for part in parts]
            ghost_left = roll(field[now, species, left, :, cells - LANES :], EY)
            ghost_right = roll(field[now, species, right, :, :LANES], -EY)
            forward = [jnp.where(left_ok, ghost_left, zero)] + [roll(part, EY) for part in parts]
            backward = [roll(part, -EY) for part in parts] + [jnp.where(right_ok, ghost_right, zero)]
            from_front = jnp.where(
                front_here, y_own[step, species, front], y_minus[step][species, front]
            )
            from_back = jnp.where(back_here, y_own[step, species, back], y_plus[step][species, back])
            from_front = jnp.where(front_ok, from_front, zero)
            from_back = jnp.where(back_ok, from_back, zero)
            ghost_y = jnp.where(even, roll(from_front, 1 - EY), roll(from_back, EY - 1))
            below = jnp.where(lower_ok, z_minus[step][species, lower], zero)
            above = jnp.where(upper_ok, z_plus[step][species, upper], zero)
            total = []
            for j in range(columns):
                part = parts[j]
                at = slice(j * LANES, (j + 1) * LANES)
                edge = jnp.concatenate(
                    [
                        roll(ghost_y, -2 * (zv * columns + j))
                        for zv in range(half // ROWS)
                    ],
                    axis=0,
                )
                value = jnp.where(below_32, forward[j], forward[j + 1])
                value = value + jnp.where(above_96, backward[j + 1], backward[j])
                value = value + jnp.where(at_low, edge, roll(part, 1))
                value = value + jnp.where(at_high, edge, roll(part, -1))
                value = value + jnp.concatenate([below[:, at], part[: half - 1]], axis=0)
                value = value + jnp.concatenate([part[1:], above[:, at]], axis=0)
                total.append(value)
            fields.append(parts)
            sums.append(total)
        amount = columns_of(dens[tile])
        share = [
            amount[j].astype(jnp.float32) / (1.0 + fields[0][j] + fields[1][j])
            for j in range(columns)
        ]
        result = []
        for species in range(2):
            rate = diffusion[species]
            keep = 1.0 - 6.0 * rate
            taken = uptake[species] * 0.125
            result.append(
                [
                    fields[species][j] * (keep - taken * share[j]) + rate * sums[species][j]
                    for j in range(columns)
                ]
            )
        return later, result

    def one_step(step):
        def body(tile, carry):
            later, result = advance(step, tile)
            for species in range(2):
                for j in range(columns):
                    at = slice(j * LANES, (j + 1) * LANES)
                    field[later, species, tile, :, at] = result[species][j]
                put_faces(step + 1, species, tile, result[species])
            return carry

        lax.fori_loop(0, slots, body, 0)

    def give(tile):
        return pltpu.make_async_remote_copy(
            src_ref=stage.at[tile], dst_ref=out.at[0, tile, own_rows, :],
            send_sem=out_send.at[tile], recv_sem=out_recv.at[tile],
            device_id=partner_id, device_id_type=MESH,
        )

    def take(tile):
        return pltpu.make_async_remote_copy(
            src_ref=stage.at[tile], dst_ref=out.at[0, tile, other_rows, :],
            send_sem=out_send.at[tile], recv_sem=out_recv.at[tile],
            device_id=partner_id, device_id_type=MESH,
        )

    for load in loads:
        load.wait()
    swap_in.wait_recv()
    lax.fori_loop(0, slots, first_faces, 0)
    send_faces(0)
    for step in range(STEPS - 1):
        wait_faces(step)
        one_step(step)
        send_faces(step + 1)
    wait_faces(STEPS - 1)

    def last_body(tile, carry):
        _, result = advance(STEPS - 1, tile)
        for j in range(columns):
            at = slice(j * LANES, (j + 1) * LANES)
            stage[tile, :, at] = jnp.where(core == 0, result[1][j], result[0][j])
        give(tile).start()
        for j in range(columns):
            at = slice(j * LANES, (j + 1) * LANES)
            out[0, tile, own_rows, at] = jnp.where(core == 0, result[0][j], result[1][j])
        return carry

    lax.fori_loop(0, slots, last_body, 0)
    swap.wait_send()
    for step in range(STEPS):
        wait_sent(step)
    for tile in range(slots):
        give(tile).wait_send()
        take(tile).wait_recv()


def per_device(layers, bands, ligand, density, counts, neighbours, diffusion, uptake):
    _, slots, depth, cells = ligand.shape
    half = depth // 2
    faces = (2, slots, ROWS, LANES)
    planes = (2, slots, 1, cells)
    smem = pl.BlockSpec(memory_space=pltpu.SMEM)
    away = pl.BlockSpec(memory_space=pl.ANY)
    return pl.pallas_call(
        functools.partial(kernel, layers, bands, slots, half, cells),
        out_shape=jax.ShapeDtypeStruct(ligand.shape, jnp.float32),
        in_specs=[smem, smem, smem, smem, away, away],
        out_specs=pl.BlockSpec(memory_space=pltpu.VMEM),
        scratch_shapes=[
            pltpu.VMEM((2, 2, slots, half, cells), jnp.float32),
            pltpu.VMEM((slots, half, cells), jnp.int32),
            pltpu.VMEM((slots, half, cells), jnp.float32),
            pltpu.VMEM((STEPS,) + faces, jnp.float32),
            [pltpu.VMEM(faces, jnp.float32)] * STEPS,
            [pltpu.VMEM(faces, jnp.float32)] * STEPS,
            pltpu.VMEM((STEPS,) + planes, jnp.float32),
            pltpu.VMEM((STEPS,) + planes, jnp.float32),
            [pltpu.VMEM(planes, jnp.float32)] * STEPS,
            [pltpu.VMEM(planes, jnp.float32)] * STEPS,
            pltpu.SemaphoreType.DMA((2,)),
            pltpu.SemaphoreType.DMA,
            pltpu.SemaphoreType.DMA,
            pltpu.SemaphoreType.DMA((STEPS, 4)),
            pltpu.SemaphoreType.DMA((STEPS, 4)),
            pltpu.SemaphoreType.DMA((slots,)),
            pltpu.SemaphoreType.DMA((slots,)),
        ],
        compiler_params=pltpu.CompilerParams(
            collective_id=0, has_side_effects=True, vmem_limit_bytes=32 * 1024 * 1024
        ),
    )(neighbours, counts, diffusion, uptake, ligand, density)


def solution(mesh):
    in_specs = (
        P("pair", ("groups", "cube", "row"), None, None),
        P(("groups", "cube", "row"), None, None),
        P(("groups", "cube", "row")),
        P(("groups", "cube", "row"), None),
        P(),
        P(),
    )
    out_specs = P("pair", ("groups", "cube", "row"), None, None)
    return jax.shard_map(
        functools.partial(per_device, mesh.shape["cube"], mesh.shape["row"]),
        mesh=mesh, in_specs=in_specs, out_specs=out_specs, check_vma=False,
    )
```

time: 94.6 us -> 29.5 us (0.31)
  starting transfers between devices: 48.1 us -> 0 us
  Pallas kernels: 0 us -> 25 us
  matrix products: 18.8 us -> 0 us
  local copies, waits for them, and re-layouts: 15.5 us -> 3.56 us
  other arithmetic: 8.82 us -> 0 us
  between operations: 2.16 us -> 0.72 us
    ppermute x20 -> x0, starting transfers between devices: 48.1 us -> none  [the longest x8 37.1 us: with_halo(): lax.ppermute(tail, axis, [(i, (i + 1) % count) for i in range(ends)])]
    pallas_call x0 -> x1, Pallas kernels: none -> 25 us  [per_device(): pl.pallas_call(functools.partial(kernel, layers, bands, slots, half, cell...]
    dot_general x48 -> x0, matrix products: 18.8 us -> none  [the longest x32 5.17 us: gather_faces(): jnp.einsum('ts,ksf->ktf', select, faces, precision=lax.Precision.HIGHEST)]
    slice x16 -> x0, local copies, waits for them, and re-layouts: 7.32 us -> none  [the longest x3 2.95 us: neighbour_sum(): z_plus = jnp.concatenate([field[:, :, 1:, :], above[:, :, None, :]], 2)]
    sub x5 -> x0, other arithmetic: 6.72 us -> none  [the longest x3 6.42 us: advance(): field + rate * (nsum - 6.0 * field)]
    another operation x36 -> x0, local copies, waits for them, and re-layouts: 3.11 us -> none
    dynamic_slice x2 -> x0, local copies, waits for them, and re-layouts: 1.22 us -> none  [the longest x1 0.61 us: per_device(): rate = lax.dynamic_slice_in_dim(diffusion, own, 1, 0).reshape(1, 1, 1, 1)]
    select_n x1 -> x0, other arithmetic: 1.15 us -> none  [per_device(): field = jnp.where(filled, ligand, jnp.float32(0.0))]
  transfers between devices with their start and end apart: 20 -> 0, of which waited for: 2 -> 0; matrix products, arithmetic and copies ran while one was open for 26% -> 0% of each run, Pallas kernels for 0% -> 0%
where the time goes in v1:
time: 29.5 us; the launch traced here: 29.2 us
  Pallas kernels  25 us (85%)
  local copies, waits for them, and re-layouts  3.56 us (12%)
  between operations  0.72 us (2%)
    pallas_call x1, Pallas kernels, per_device(): pl.pallas_call(functools.partial(kernel, layers, bands, slots, half, cell...  25 us
    unnamed x11, local copies, waits for them, and re-layouts  3.56 us

profile of v1, /device:TPU:0, one launch (start us, length us, event | category | flops | bytes accessed | tf_op | source)
XLA Modules:
  0.0 29.2 jit_solution(13522694495179448313)
XLA Ops:
  0.0 0.0 copy-start.4
  0.0 0.0 copy-start.3
  0.7 0.0 copy-done.4
  0.7 0.0 copy-done.3
  0.7 0.0 copy-start
  0.7 1.0 %copy-done = f32[1,4,32,1024]{3,2,1,0:T(8,128)S(1)} copy-done((f32[1,4,32,1024]{3,2,1,0:T(8,128)S(1)}, f32[1,4,32,1024]{3,2,1,0:T(8,128)}, u32[]{:S(2)}) %copy-start) | copy-done | bytes 524312
  1.7 0.0 copy-start.1
  1.7 1.0 %copy-done.1 = s32[4,32,1024]{2,1,0:T(8,128)S(1)} copy-done((s32[4,32,1024]{2,1,0:T(8,128)S(1)}, s32[4,32,1024]{2,1,0:T(8,128)}, u32[]{:S(2)}) %copy-start.1) | copy-done | bytes 524312
  2.8 0.0 copy-start.2
  2.8 0.7 %copy-done.2 = s32[4,6]{1,0:T(4,128)S(1)} copy-done((s32[4,6]{1,0:T(4,128)S(1)}, s32[4,6]{1,0:T(4,128)}, u32[]{:S(2)}) %copy-start.2) | copy-done | bytes 120
  3.5 25.0 %shard_map.64 = f32[1,4,32,1024]{3,2,1,0:T(8,128)S(1)} custom-call(s32[4,6]{1,0:T(4,128)S(1)} %copy-done.2, s32[1]{0:T(128)S(6)} %copy.8.counts, f32[2]{0:T(128)S(1)} %copy-done.3, f32[2]{0:T(128)S(1)} %copy-done.4, f32[1,4,32,1024]{3,2,1,0:T(8,128)S(1)} %copy-done, s32[4,32,1024]{2,1,0:T(8,128)S(1)} %copy-done.1), custom_call_target="tpu_custom_call" | custom-call | tf_op jit(solution)/shard_map/pallas_call | solution.py:291
  28.5 0.8 %copy.9 = f32[1,4,32,1024]{3,2,1,0:T(8,128)} copy(f32[1,4,32,1024]{3,2,1,0:T(8,128)S(1)} %shard_map.64) | data formatting | bytes 1048576
Async XLA Ops:
  0.0 0.7 %copy-start.4 = (f32[2]{0:T(128)S(1)}, f32[2]{0:T(128)}, u32[]{:S(2)}) copy-start(f32[2]{0:T(128)} %uptake.1) | copy-start | bytes 28
  0.0 0.7 %copy-start.3 = (f32[2]{0:T(128)S(1)}, f32[2]{0:T(128)}, u32[]{:S(2)}) copy-start(f32[2]{0:T(128)} %diffusion.1) | copy-start | bytes 28
  0.7 1.0 %copy-start = (f32[1,4,32,1024]{3,2,1,0:T(8,128)S(1)}, f32[1,4,32,1024]{3,2,1,0:T(8,128)}, u32[]{:S(2)}) copy-start(f32[1,4,32,1024]{3,2,1,0:T(8,128)} %ligand.1) | copy-start | bytes 1572868
  1.7 1.0 %copy-start.1 = (s32[4,32,1024]{2,1,0:T(8,128)S(1)}, s32[4,32,1024]{2,1,0:T(8,128)}, u32[]{:S(2)}) copy-start(s32[4,32,1024]{2,1,0:T(8,128)} %density.1) | copy-start | bytes 1572868
  2.8 0.7 %copy-start.2 = (s32[4,6]{1,0:T(4,128)S(1)}, s32[4,6]{1,0:T(4,128)}, u32[]{:S(2)}) copy-start(s32[4,6]{1,0:T(4,128)} %nbr.1) | copy-start | bytes 292

commit v2 on v1

--- a/solution.py
+++ b/solution.py
@@ -17,7 +17,7 @@
 def kernel(
     layers, bands, slots, half, cells,
     nbr, counts, diffusion, uptake, ligand, density, out,
-    field, dens, stage, y_own, y_minus, y_plus, z_low, z_high, z_minus, z_plus,
+    field, dens, stage, y_high, y_low, y_minus, y_plus, z_low, z_high, z_minus, z_plus,
     load_sem, swap_send, swap_recv, face_send, face_recv, out_send, out_recv,
 ):
     core = lax.axis_index("pair")
@@ -85,8 +85,8 @@
         up_near = remote(z_high, z_minus, step, 0, partner_id)
         down_far = remote(z_low, z_plus, step, 1, far_id)
         down_near = remote(z_low, z_plus, step, 1, partner_id)
-        to_plus = remote(y_own, y_minus, step, 2, plus_id)
-        to_minus = remote(y_own, y_plus, step, 3, minus_id)
+        to_plus = remote(y_high, y_minus, step, 2, plus_id)
+        to_minus = remote(y_low, y_plus, step, 3, minus_id)
         both = jnp.logical_and
         sends = [
             (both(last, has_far), up_far), (first, up_near),
@@ -117,6 +117,7 @@
     wide = lax.broadcasted_iota(jnp.int32, (half, LANES), 1)
     at_low = lax.rem(wide, EY) == 0
     at_high = lax.rem(wide, EY) == EY - 1
+    at_edge = jnp.logical_or(at_low, at_high)
     below_32 = wide < EY
     above_96 = wide >= LANES - EY
 
@@ -126,115 +127,134 @@
 
     pieces = [(zv, j) for zv in range(half // ROWS) for j in range(columns)]
 
-    def put_faces(step, species, tile, parts):
-        packed = None
-        for m, (zv, j) in enumerate(pieces):
-            piece = roll(parts[j][zv * ROWS : (zv + 1) * ROWS], 2 * m)
-            packed = piece if packed is None else jnp.where(pair_of == m, piece, packed)
-        y_own[step, species, tile] = packed
-        for j in range(columns):
-            at = slice(j * LANES, (j + 1) * LANES)
-            z_low[step, species, tile, :, at] = parts[j][:1]
-            z_high[step, species, tile, :, at] = parts[j][half - 1 :]
+    def put_faces(step, tile, both):
+        packed = []
+        for species in range(2):
+            parts = both[species]
+            total = None
+            for m, (zv, j) in enumerate(pieces):
+                piece = roll(parts[j][zv * ROWS : (zv + 1) * ROWS], 2 * m)
+                total = piece if total is None else jnp.where(pair_of == m, piece, total)
+            packed.append(total)
+            for j in range(columns):
+                at = slice(j * LANES, (j + 1) * LANES)
+                z_low[step, species, tile, :, at] = parts[j][:1]
+                z_high[step, species, tile, :, at] = parts[j][half - 1 :]
+        second = roll(packed[1], 1)
+        y_low[step, tile] = jnp.where(even, packed[0], second)
+        y_high[step, tile] = jnp.where(even, second, packed[0])
 
     def columns_of(value):
         return [value[:, j * LANES : (j + 1) * LANES] for j in range(columns)]
 
     def first_faces(tile, carry):
-        for species in range(2):
-            put_faces(0, species, tile, columns_of(field[0, species, tile]))
+        put_faces(0, tile, [columns_of(field[0, species, tile]) for species in range(2)])
         return carry
 
     zero = jnp.float32(0.0)
-
-    def advance(step, tile):
+    row = lax.broadcasted_iota(jnp.int32, (half, LANES), 0)
+
+    def entry(tile, k):
+        value = nbr[tile, k]
+        safe = jnp.maximum(value, 0)
+        return value >= 0, lax.rem(safe, slots), safe // slots == block
+
+    def inner(step, tile):
         now, later = step % 2, (step + 1) % 2
         filled = tile < counts[0]
-
-        def entry(k):
-            value = nbr[tile, k]
-            safe = jnp.maximum(value, 0)
-            return value >= 0, lax.rem(safe, slots), safe // slots == block
-
-        left_ok, left, _ = entry(0)
-        right_ok, right, _ = entry(1)
-        front_ok, front, front_here = entry(2)
-        back_ok, back, back_here = entry(3)
-        lower_ok, lower, _ = entry(4)
-        upper_ok, upper, _ = entry(5)
+        left_ok, left, _ = entry(tile, 0)
+        right_ok, right, _ = entry(tile, 1)
+        fields = []
+        for species in range(2):
+            parts = columns_of(field[now, species, tile])
+            if step == 0:
+                parts = [jnp.where(filled, part, zero) for part in parts]
+            fields.append(parts)
+        amount = columns_of(dens[tile])
+        share = [
+            amount[j].astype(jnp.float32) / (1.0 + fields[0][j] + fields[1][j])
+            for j in range(columns)
+        ]
+        blank = jnp.zeros((1, LANES), jnp.float32)
+        for species in range(2):
+            parts = fields[species]
+            rate = diffusion[species]
+            keep = 1.0 - 6.0 * rate
+            taken = uptake[species] * 0.125
+            ghost_left = roll(field[now, species, left, :, cells - LANES :], EY)
+            ghost_right = roll(field[now, species, right, :, :LANES], -EY)
+            forward = [jnp.where(left_ok, ghost_left, zero)] + [roll(part, EY) for part in parts]
+            backward = [roll(part, -EY) for part in parts] + [jnp.where(right_ok, ghost_right, zero)]
+            for j in range(columns):
+                part = parts[j]
+                value = jnp.where(below_32, forward[j], forward[j + 1])
+                value = value + jnp.where(above_96, backward[j + 1], backward[j])
+                value = value + jnp.where(at_low, zero, roll(part, 1))
+                value = value + jnp.where(at_high, zero, roll(part, -1))
+                value = value + jnp.concatenate([blank, part[: half - 1]], axis=0)
+                value = value + jnp.concatenate([part[1:], blank], axis=0)
+                at = slice(j * LANES, (j + 1) * LANES)
+                field[later, species, tile, :, at] = (
+                    part * (keep - taken * share[j]) + rate * value
+                )
+
+    def outer(step, tile):
+        later = (step + 1) % 2
+        filled = tile < counts[0]
+        front_ok, front, front_here = entry(tile, 2)
+        back_ok, back, back_here = entry(tile, 3)
+        lower_ok, lower, _ = entry(tile, 4)
+        upper_ok, upper, _ = entry(tile, 5)
         first = core == 0
         lower = jnp.where(first, lower, tile)
         lower_ok = jnp.where(first, lower_ok, filled)
         upper = jnp.where(first, tile, upper)
         upper_ok = jnp.where(first, filled, upper_ok)
-
-        fields, sums = [], []
-        for species in range(2):
-            parts = columns_of(field[now, species, tile])
-            if step == 0:
-                parts = [jnp.where(filled, part, zero) for part in parts]
-            ghost_left = roll(field[now, species, left, :, cells - LANES :], EY)
-            ghost_right = roll(field[now, species, right, :, :LANES], -EY)
-            forward = [jnp.where(left_ok, ghost_left, zero)] + [roll(part, EY) for part in parts]
-            backward = [roll(part, -EY) for part in parts] + [jnp.where(right_ok, ghost_right, zero)]
-            from_front = jnp.where(
-                front_here, y_own[step, species, front], y_minus[step][species, front]
-            )
-            from_back = jnp.where(back_here, y_own[step, species, back], y_plus[step][species, back])
-            from_front = jnp.where(front_ok, from_front, zero)
-            from_back = jnp.where(back_ok, from_back, zero)
-            ghost_y = jnp.where(even, roll(from_front, 1 - EY), roll(from_back, EY - 1))
-            below = jnp.where(lower_ok, z_minus[step][species, lower], zero)
-            above = jnp.where(upper_ok, z_plus[step][species, upper], zero)
-            total = []
-            for j in range(columns):
-                part = parts[j]
-                at = slice(j * LANES, (j + 1) * LANES)
-                edge = jnp.concatenate(
-                    [
-                        roll(ghost_y, -2 * (zv * columns + j))
-                        for zv in range(half // ROWS)
-                    ],
-                    axis=0,
-                )
-                value = jnp.where(below_32, forward[j], forward[j + 1])
-                value = value + jnp.where(above_96, backward[j + 1], backward[j])
-                value = value + jnp.where(at_low, edge, roll(part, 1))
-                value = value + jnp.where(at_high, edge, roll(part, -1))
-                value = value + jnp.concatenate([below[:, at], part[: half - 1]], axis=0)
-                value = value + jnp.concatenate([part[1:], above[:, at]], axis=0)
-                total.append(value)
-            fields.append(parts)
-            sums.append(total)
-        amount = columns_of(dens[tile])
-        share = [
-            amount[j].astype(jnp.float32) / (1.0 + fields[0][j] + fields[1][j])
-            for j in range(columns)
-        ]
+        from_front = jnp.where(front_here, y_high[step, front], y_minus[step][front])
+        from_back = jnp.where(back_here, y_low[step, back], y_plus[step][back])
+        from_front = jnp.where(front_ok, from_front, zero)
+        from_back = jnp.where(back_ok, from_back, zero)
         result = []
         for species in range(2):
             rate = diffusion[species]
-            keep = 1.0 - 6.0 * rate
-            taken = uptake[species] * 0.125
-            result.append(
-                [
-                    fields[species][j] * (keep - taken * share[j]) + rate * sums[species][j]
-                    for j in range(columns)
-                ]
+            ghost_y = rate * jnp.where(
+                even, roll(from_front, 1 - EY - species), roll(from_back, EY - 1 - species)
             )
-        return later, result
-
-    def one_step(step):
+            below = rate * jnp.where(lower_ok, z_minus[step][species, lower], zero)
+            above = rate * jnp.where(upper_ok, z_plus[step][species, upper], zero)
+            values = []
+            for j in range(columns):
+                at = slice(j * LANES, (j + 1) * LANES)
+                edge = jnp.concatenate(
+                    [roll(ghost_y, -2 * (zv * columns + j)) for zv in range(half // ROWS)], axis=0
+                )
+                value = field[later, species, tile, :, at] + jnp.where(at_edge, edge, zero)
+                value = value + jnp.where(row == 0, below[:, at], zero)
+                value = value + jnp.where(row == half - 1, above[:, at], zero)
+                values.append(value)
+            result.append(values)
+        return result
+
+    def inner_step(step):
         def body(tile, carry):
-            later, result = advance(step, tile)
+            inner(step, tile)
+            return carry
+
+        lax.fori_loop(0, slots, body, 0, unroll=True)
+
+    def outer_step(step):
+        later = (step + 1) % 2
+
+        def body(tile, carry):
+            result = outer(step, tile)
             for species in range(2):
                 for j in range(columns):
                     at = slice(j * LANES, (j + 1) * LANES)
                     field[later, species, tile, :, at] = result[species][j]
-                put_faces(step + 1, species, tile, result[species])
+            put_faces(step + 1, tile, result)
             return carry
 
-        lax.fori_loop(0, slots, body, 0)
+        lax.fori_loop(0, slots, body, 0, unroll=True)
 
     def give(tile):
         return pltpu.make_async_remote_copy(
@@ -256,13 +276,15 @@
     lax.fori_loop(0, slots, first_faces, 0)
     send_faces(0)
     for step in range(STEPS - 1):
+        inner_step(step)
         wait_faces(step)
-        one_step(step)
+        outer_step(step)
         send_faces(step + 1)
+    inner_step(STEPS - 1)
     wait_faces(STEPS - 1)
 
     def last_body(tile, carry):
-        _, result = advance(STEPS - 1, tile)
+        result = outer(STEPS - 1, tile)
         for j in range(columns):
             at = slice(j * LANES, (j + 1) * LANES)
             stage[tile, :, at] = jnp.where(core == 0, result[1][j], result[0][j])
@@ -284,10 +306,10 @@
 def per_device(layers, bands, ligand, density, counts, neighbours, diffusion, uptake):
     _, slots, depth, cells = ligand.shape
     half = depth // 2
-    faces = (2, slots, ROWS, LANES)
+    faces = (slots, ROWS, LANES)
     planes = (2, slots, 1, cells)
     smem = pl.BlockSpec(memory_space=pltpu.SMEM)
-    away = pl.BlockSpec(memory_space=pl.ANY)
+    away = pl.BlockSpec(memory_space=pltpu.HBM)
     return pl.pallas_call(
         functools.partial(kernel, layers, bands, slots, half, cells),
         out_shape=jax.ShapeDtypeStruct(ligand.shape, jnp.float32),
@@ -297,6 +319,7 @@
             pltpu.VMEM((2, 2, slots, half, cells), jnp.float32),
             pltpu.VMEM((slots, half, cells), jnp.int32),
             pltpu.VMEM((slots, half, cells), jnp.float32),
+            pltpu.VMEM((STEPS,) + faces, jnp.float32),
             pltpu.VMEM((STEPS,) + faces, jnp.float32),
             [pltpu.VMEM(faces, jnp.float32)] * STEPS,
             [pltpu.VMEM(faces, jnp.float32)] * STEPS,
@@ -313,7 +336,7 @@
             pltpu.SemaphoreType.DMA((slots,)),
         ],
         compiler_params=pltpu.CompilerParams(
-            collective_id=0, has_side_effects=True, vmem_limit_bytes=32 * 1024 * 1024
+            collective_id=0, has_side_effects=True, vmem_limit_bytes=56 * 1024 * 1024
         ),
     )(neighbours, counts, diffusion, uptake, ligand, density)
 

time: 29.5 us -> 25.4 us (0.86)
  Pallas kernels: 25 us -> 22.7 us
  local copies, waits for them, and re-layouts: 3.56 us -> 1.89 us
    pallas_call x1, Pallas kernels: 25 us -> 22.7 us  [per_device(): pl.pallas_call(functools.partial(kernel, layers, bands, slots, half, cell...]
    unnamed x11 -> x1, local copies, waits for them, and re-layouts: 3.56 us -> 1.89 us
where the time goes in v2:
time: 25.4 us; the launch traced here: 25.2 us
  Pallas kernels  22.7 us (89%)
  local copies, waits for them, and re-layouts  1.89 us (7%)
  between operations  0.66 us (3%)
    pallas_call x1, Pallas kernels, per_device(): pl.pallas_call(functools.partial(kernel, layers, bands, slots, half, cell...  22.7 us
    unnamed x1, local copies, waits for them, and re-layouts  1.89 us

profile of v2, /device:TPU:0, one launch (start us, length us, event | category | flops | bytes accessed | tf_op | source)
XLA Modules:
  0.0 25.2 jit_solution(9486973245352387991)
XLA Ops:
  0.7 22.7 %shard_map.64 = f32[1,4,32,1024]{3,2,1,0:T(8,128)} custom-call(s32[4,6]{1,0:T(4,128)} %nbr.1, s32[1]{0:T(128)S(6)} %copy.8.counts, f32[2]{0:T(128)} %diffusion.1, f32[2]{0:T(128)} %uptake.1, f32[1,4,32,1024]{3,2,1,0:T(8,128)} %ligand.1, s32[4,32,1024]{2,1,0:T(8,128)} %density.1), custom_call_target="tpu_custom_call" | custom-call | tf_op jit(solution)/shard_map/pallas_call | solution.py:313
  23.3 1.9 %copy.9 = f32[1,4,32,1024]{3,2,1,0:T(8,128)} copy(f32[1,4,32,1024]{3,2,1,0:T(8,128)} %shard_map.64) | data formatting | bytes 1048576

commit v3 on v2

--- a/solution.py
+++ b/solution.py
@@ -18,6 +18,7 @@
     layers, bands, slots, half, cells,
     nbr, counts, diffusion, uptake, ligand, density, out,
     field, dens, stage, y_high, y_low, y_minus, y_plus, z_low, z_high, z_minus, z_plus,
+    extra, y_first, y_here, z_first_low, z_first_high, first_send, first_recv,
     load_sem, swap_send, swap_recv, face_send, face_recv, out_send, out_recv,
 ):
     core = lax.axis_index("pair")
@@ -39,27 +40,34 @@
     other_rows = pl.ds(pl.multiple_of(other * half, half), half)
     loads = [
         pltpu.make_async_copy(ligand.at[0, :, own_rows, :], field.at[0, core], load_sem.at[0]),
+        pltpu.make_async_copy(ligand.at[0, :, other_rows, :], extra, load_sem.at[2]),
         pltpu.make_async_copy(density.at[:, own_rows, :], dens, load_sem.at[1]),
     ]
     for load in loads:
         load.start()
 
     barrier = pltpu.get_barrier_semaphore()
-    pl.semaphore_signal(barrier, inc=1, device_id=partner_id, device_id_type=MESH)
-
-    @pl.when(has_far)
-    def _():
-        pl.semaphore_signal(barrier, inc=1, device_id=far_id, device_id_type=MESH)
-
-    @pl.when(has_minus)
-    def _():
-        pl.semaphore_signal(barrier, inc=1, device_id=minus_id, device_id_type=MESH)
-
-    @pl.when(has_plus)
-    def _():
-        pl.semaphore_signal(barrier, inc=1, device_id=plus_id, device_id_type=MESH)
-
-    peers = 1 + has_far.astype(jnp.int32) + has_minus.astype(jnp.int32) + has_plus.astype(jnp.int32)
+    has_down = layer > 0
+    has_up = layer < layers - 1
+    always = layer >= 0
+    greeted = [
+        (always, partner_id),
+        (has_far, far_id),
+        (has_down, {"cube": layer - 1}),
+        (has_up, {"cube": layer + 1}),
+        (has_minus, minus_id),
+        (has_plus, plus_id),
+        (has_minus, {"row": band - 1, "pair": other}),
+        (has_plus, {"row": band + 1, "pair": other}),
+    ]
+    peers = jnp.int32(0)
+    for wanted, device in greeted:
+        pl.when(wanted)(
+            functools.partial(
+                pl.semaphore_signal, barrier, inc=1, device_id=device, device_id_type=MESH
+            )
+        )
+        peers = peers + wanted.astype(jnp.int32)
     pl.semaphore_wait(barrier, peers)
 
     swap = pltpu.make_async_remote_copy(
@@ -99,6 +107,49 @@
         ]
         return sends, receives
 
+    def first_copy(source, target, k, at, device):
+        return pltpu.make_async_remote_copy(
+            src_ref=source, dst_ref=target.at[core],
+            send_sem=first_send.at[k], recv_sem=first_recv.at[at, core],
+            device_id=device, device_id_type=MESH,
+        )
+
+    def first_sends():
+        return [
+            (core == 0, first_copy(z_first_high.at[0], z_minus[0], 0, 0, partner_id)),
+            (core == 1, first_copy(z_first_low.at[1], z_plus[0], 1, 1, partner_id)),
+            (has_down, first_copy(
+                z_first_low.at[0], z_plus[0], 2, 1, {"cube": layer - 1, "pair": core * 0 + 1})),
+            (has_up, first_copy(
+                z_first_high.at[1], z_minus[0], 3, 0, {"cube": layer + 1, "pair": core * 0})),
+        ] + [
+            (has_plus, first_copy(
+                y_first.at[h], y_minus[0], 4 + h, 2, {"row": band + 1, "pair": core * 0 + h}))
+            for h in range(2)
+        ] + [
+            (has_minus, first_copy(
+                y_first.at[h], y_plus[0], 6 + h, 3, {"row": band - 1, "pair": core * 0 + h}))
+            for h in range(2)
+        ]
+
+    def arrived(target, at, species):
+        pltpu.make_async_remote_copy(
+            src_ref=target.at[species], dst_ref=target.at[species],
+            send_sem=first_send.at[0], recv_sem=first_recv.at[at, species],
+            device_id=partner_id, device_id_type=MESH,
+        ).wait_recv()
+
+    def wait_first():
+        both, either = jnp.logical_and, jnp.logical_or
+        for species in range(2):
+            across = core == 1 - species
+            minus = either(both(core == 0, has_down), both(core == 1, across))
+            plus = either(both(core == 1, has_up), both(core == 0, across))
+            pl.when(minus)(functools.partial(arrived, z_minus[0], 0, species))
+            pl.when(plus)(functools.partial(arrived, z_plus[0], 1, species))
+            pl.when(has_minus)(functools.partial(arrived, y_minus[0], 2, species))
+            pl.when(has_plus)(functools.partial(arrived, y_plus[0], 3, species))
+
     def send_faces(step):
         for wanted, copy in messages(step)[0]:
             pl.when(wanted)(copy.start)
@@ -127,15 +178,18 @@
 
     pieces = [(zv, j) for zv in range(half // ROWS) for j in range(columns)]
 
+    def pack(parts):
+        total = None
+        for m, (zv, j) in enumerate(pieces):
+            piece = roll(parts[j][zv * ROWS : (zv + 1) * ROWS], 2 * m)
+            total = piece if total is None else jnp.where(pair_of == m, piece, total)
+        return total
+
     def put_faces(step, tile, both):
         packed = []
         for species in range(2):
             parts = both[species]
-            total = None
-            for m, (zv, j) in enumerate(pieces):
-                piece = roll(parts[j][zv * ROWS : (zv + 1) * ROWS], 2 * m)
-                total = piece if total is None else jnp.where(pair_of == m, piece, total)
-            packed.append(total)
+            packed.append(pack(parts))
             for j in range(columns):
                 at = slice(j * LANES, (j + 1) * LANES)
                 z_low[step, species, tile, :, at] = parts[j][:1]
@@ -148,8 +202,27 @@
         return [value[:, j * LANES : (j + 1) * LANES] for j in range(columns)]
 
     def first_faces(tile, carry):
-        put_faces(0, tile, [columns_of(field[0, species, tile]) for species in range(2)])
+        for h, value in ((core, field[0, core, tile]), (other, extra[tile])):
+            packed = pack(columns_of(value))
+            y_first[h, tile] = packed
+            z_first_low[h, tile] = value[:1]
+            z_first_high[h, tile] = value[half - 1 :]
+            if h is core:
+                y_here[core, tile] = packed
         return carry
+
+    def other_faces(tile, carry):
+        y_here[other, tile] = pack(columns_of(field[0, other, tile]))
+        return carry
+
+    def own_planes():
+        @pl.when(core == 0)
+        def _():
+            z_plus[0][0] = z_first_low[1]
+
+        @pl.when(core == 1)
+        def _():
+            z_minus[0][1] = z_first_high[0]
 
     zero = jnp.float32(0.0)
     row = lax.broadcasted_iota(jnp.int32, (half, LANES), 0)
@@ -210,15 +283,21 @@
         lower_ok = jnp.where(first, lower_ok, filled)
         upper = jnp.where(first, tile, upper)
         upper_ok = jnp.where(first, filled, upper_ok)
-        from_front = jnp.where(front_here, y_high[step, front], y_minus[step][front])
-        from_back = jnp.where(back_here, y_low[step, back], y_plus[step][back])
-        from_front = jnp.where(front_ok, from_front, zero)
-        from_back = jnp.where(back_ok, from_back, zero)
         result = []
         for species in range(2):
             rate = diffusion[species]
+            if step == 0:
+                shift = 0
+                from_front = jnp.where(front_here, y_here[species, front], y_minus[0][species, front])
+                from_back = jnp.where(back_here, y_here[species, back], y_plus[0][species, back])
+            else:
+                shift = species
+                from_front = jnp.where(front_here, y_high[step, front], y_minus[step][front])
+                from_back = jnp.where(back_here, y_low[step, back], y_plus[step][back])
+            from_front = jnp.where(front_ok, from_front, zero)
+            from_back = jnp.where(back_ok, from_back, zero)
             ghost_y = rate * jnp.where(
-                even, roll(from_front, 1 - EY - species), roll(from_back, EY - 1 - species)
+                even, roll(from_front, 1 - EY - shift), roll(from_back, EY - 1 - shift)
             )
             below = rate * jnp.where(lower_ok, z_minus[step][species, lower], zero)
             above = rate * jnp.where(upper_ok, z_plus[step][species, upper], zero)
@@ -270,18 +349,24 @@
             device_id=partner_id, device_id_type=MESH,
         )
 
-    for load in loads:
-        load.wait()
+    loads[0].wait()
+    loads[1].wait()
+    lax.fori_loop(0, slots, first_faces, 0, unroll=True)
+    for wanted, copy in first_sends():
+        pl.when(wanted)(copy.start)
+    own_planes()
+    loads[2].wait()
     swap_in.wait_recv()
-    lax.fori_loop(0, slots, first_faces, 0)
-    send_faces(0)
-    for step in range(STEPS - 1):
+    lax.fori_loop(0, slots, other_faces, 0, unroll=True)
+    for step in range(STEPS):
         inner_step(step)
-        wait_faces(step)
-        outer_step(step)
-        send_faces(step + 1)
-    inner_step(STEPS - 1)
-    wait_faces(STEPS - 1)
+        if step == 0:
+            wait_first()
+        else:
+            wait_faces(step)
+        if step < STEPS - 1:
+            outer_step(step)
+            send_faces(step + 1)
 
     def last_body(tile, carry):
         result = outer(STEPS - 1, tile)
@@ -296,7 +381,9 @@
 
     lax.fori_loop(0, slots, last_body, 0)
     swap.wait_send()
-    for step in range(STEPS):
+    for wanted, copy in first_sends():
+        pl.when(wanted)(copy.wait_send)
+    for step in range(1, STEPS):
         wait_sent(step)
     for tile in range(slots):
         give(tile).wait_send()
@@ -321,13 +408,20 @@
             pltpu.VMEM((slots, half, cells), jnp.float32),
             pltpu.VMEM((STEPS,) + faces, jnp.float32),
             pltpu.VMEM((STEPS,) + faces, jnp.float32),
-            [pltpu.VMEM(faces, jnp.float32)] * STEPS,
-            [pltpu.VMEM(faces, jnp.float32)] * STEPS,
+            [pltpu.VMEM((2,) + faces, jnp.float32)] + [pltpu.VMEM(faces, jnp.float32)] * (STEPS - 1),
+            [pltpu.VMEM((2,) + faces, jnp.float32)] + [pltpu.VMEM(faces, jnp.float32)] * (STEPS - 1),
             pltpu.VMEM((STEPS,) + planes, jnp.float32),
             pltpu.VMEM((STEPS,) + planes, jnp.float32),
             [pltpu.VMEM(planes, jnp.float32)] * STEPS,
             [pltpu.VMEM(planes, jnp.float32)] * STEPS,
-            pltpu.SemaphoreType.DMA((2,)),
+            pltpu.VMEM((slots, half, cells), jnp.float32),
+            pltpu.VMEM((2,) + faces, jnp.float32),
+            pltpu.VMEM((2,) + faces, jnp.float32),
+            pltpu.VMEM(planes, jnp.float32),
+            pltpu.VMEM(planes, jnp.float32),
+            pltpu.SemaphoreType.DMA((8,)),
+            pltpu.SemaphoreType.DMA((4, 2)),
+            pltpu.SemaphoreType.DMA((3,)),
             pltpu.SemaphoreType.DMA,
             pltpu.SemaphoreType.DMA,
             pltpu.SemaphoreType.DMA((STEPS, 4)),
@@ -336,7 +430,7 @@
             pltpu.SemaphoreType.DMA((slots,)),
         ],
         compiler_params=pltpu.CompilerParams(
-            collective_id=0, has_side_effects=True, vmem_limit_bytes=56 * 1024 * 1024
+            collective_id=0, has_side_effects=True, vmem_limit_bytes=53 * 1024 * 1024
         ),
     )(neighbours, counts, diffusion, uptake, ligand, density)
 

time: 25.4 us -> 22.6 us (0.89)
  Pallas kernels: 22.7 us -> 20.2 us
  local copies, waits for them, and re-layouts: 1.89 us -> 1.48 us
    pallas_call x1, Pallas kernels: 22.7 us -> 20.2 us  [per_device(): pl.pallas_call(functools.partial(kernel, layers, bands, slots, half, cell...]
    unnamed x1 -> x7, local copies, waits for them, and re-layouts: 1.89 us -> 1.48 us
where the time goes in v3:
time: 22.6 us; the launch traced here: 22.4 us
  Pallas kernels  20.2 us (89%)
  local copies, waits for them, and re-layouts  1.48 us (7%)
  between operations  0.71 us (3%)
    pallas_call x1, Pallas kernels, per_device(): pl.pallas_call(functools.partial(kernel, layers, bands, slots, half, cell...  20.2 us
    unnamed x7, local copies, waits for them, and re-layouts  1.48 us

profile of v3, /device:TPU:0, one launch (start us, length us, event | category | flops | bytes accessed | tf_op | source)
XLA Modules:
  0.0 22.4 jit_solution(4285013028454019971)
XLA Ops:
  0.0 0.0 copy-start.2
  0.0 0.0 copy-start.1
  0.7 0.0 copy-done.2
  0.7 0.0 copy-done.1
  0.7 0.0 copy-start
  0.7 0.7 %copy-done = s32[4,6]{1,0:T(4,128)S(1)} copy-done((s32[4,6]{1,0:T(4,128)S(1)}, s32[4,6]{1,0:T(4,128)}, u32[]{:S(2)}) %copy-start) | copy-done | bytes 120
  1.4 20.2 %shard_map.64 = f32[1,4,32,1024]{3,2,1,0:T(8,128)S(1)} custom-call(s32[4,6]{1,0:T(4,128)S(1)} %copy-done, s32[1]{0:T(128)S(6)} %copy.8.counts, f32[2]{0:T(128)S(1)} %copy-done.1, f32[2]{0:T(128)S(1)} %copy-done.2, f32[1,4,32,1024]{3,2,1,0:T(8,128)} %ligand.1, s32[4,32,1024]{2,1,0:T(8,128)} %density.1), custom_call_target="tpu_custom_call" | custom-call | tf_op jit(solution)/shard_map/pallas_call | solution.py:400
  21.6 0.8 %copy.9 = f32[1,4,32,1024]{3,2,1,0:T(8,128)} copy(f32[1,4,32,1024]{3,2,1,0:T(8,128)S(1)} %shard_map.64) | data formatting | bytes 1048576
Async XLA Ops:
  0.0 0.7 %copy-start.2 = (f32[2]{0:T(128)S(1)}, f32[2]{0:T(128)}, u32[]{:S(2)}) copy-start(f32[2]{0:T(128)} %uptake.1) | copy-start | bytes 28
  0.0 0.7 %copy-start.1 = (f32[2]{0:T(128)S(1)}, f32[2]{0:T(128)}, u32[]{:S(2)}) copy-start(f32[2]{0:T(128)} %diffusion.1) | copy-start | bytes 28
  0.7 0.7 %copy-start = (s32[4,6]{1,0:T(4,128)S(1)}, s32[4,6]{1,0:T(4,128)}, u32[]{:S(2)}) copy-start(s32[4,6]{1,0:T(4,128)} %nbr.1) | copy-start | bytes 292

commit v4 on v3

--- a/solution.py
+++ b/solution.py
@@ -97,9 +97,9 @@
         to_minus = remote(y_low, y_plus, step, 3, minus_id)
         both = jnp.logical_and
         sends = [
-            (both(last, has_far), up_far), (first, up_near),
-            (both(first, has_far), down_far), (last, down_near),
             (has_plus, to_plus), (has_minus, to_minus),
+            (both(last, has_far), up_far), (both(first, has_far), down_far),
+            (first, up_near), (last, down_near),
         ]
         receives = [
             (jnp.logical_or(last, has_far), up_near), (jnp.logical_or(first, has_far), down_near),
@@ -319,7 +319,7 @@
             inner(step, tile)
             return carry
 
-        lax.fori_loop(0, slots, body, 0, unroll=True)
+        lax.fori_loop(0, slots, body, 0)
 
     def outer_step(step):
         later = (step + 1) % 2
@@ -379,7 +379,7 @@
             out[0, tile, own_rows, at] = jnp.where(core == 0, result[0][j], result[1][j])
         return carry
 
-    lax.fori_loop(0, slots, last_body, 0)
+    lax.fori_loop(0, slots, last_body, 0, unroll=True)
     swap.wait_send()
     for wanted, copy in first_sends():
         pl.when(wanted)(copy.wait_send)

time: 22.6 us -> 21.6 us (0.956)
  Pallas kernels: 20.2 us -> 19.2 us
    pallas_call x1, Pallas kernels: 20.2 us -> 19.2 us  [per_device(): pl.pallas_call(functools.partial(kernel, layers, bands, slots, half, cell...]
where the time goes in v4:
time: 21.6 us; the launch traced here: 21.4 us
  Pallas kernels  19.2 us (89%)
  local copies, waits for them, and re-layouts  1.48 us (7%)
  between operations  0.71 us (3%)
    pallas_call x1, Pallas kernels, per_device(): pl.pallas_call(functools.partial(kernel, layers, bands, slots, half, cell...  19.2 us
    unnamed x7, local copies, waits for them, and re-layouts  1.48 us

profile of v4, /device:TPU:0, one launch (start us, length us, event | category | flops | bytes accessed | tf_op | source)
XLA Modules:
  0.0 21.4 jit_solution(1177733410883720034)
XLA Ops:
  0.0 0.0 copy-start.2
  0.0 0.0 copy-start.1
  0.7 0.0 copy-done.2
  0.7 0.0 copy-done.1
  0.7 0.0 copy-start
  0.7 0.7 %copy-done = s32[4,6]{1,0:T(4,128)S(1)} copy-done((s32[4,6]{1,0:T(4,128)S(1)}, s32[4,6]{1,0:T(4,128)}, u32[]{:S(2)}) %copy-start) | copy-done | bytes 120
  1.4 19.2 %shard_map.64 = f32[1,4,32,1024]{3,2,1,0:T(8,128)S(1)} custom-call(s32[4,6]{1,0:T(4,128)S(1)} %copy-done, s32[1]{0:T(128)S(6)} %copy.8.counts, f32[2]{0:T(128)S(1)} %copy-done.1, f32[2]{0:T(128)S(1)} %copy-done.2, f32[1,4,32,1024]{3,2,1,0:T(8,128)} %ligand.1, s32[4,32,1024]{2,1,0:T(8,128)} %density.1), custom_call_target="tpu_custom_call" | custom-call | tf_op jit(solution)/shard_map/pallas_call | solution.py:400
  20.6 0.8 %copy.9 = f32[1,4,32,1024]{3,2,1,0:T(8,128)} copy(f32[1,4,32,1024]{3,2,1,0:T(8,128)S(1)} %shard_map.64) | data formatting | bytes 1048576
Async XLA Ops:
  0.0 0.7 %copy-start.2 = (f32[2]{0:T(128)S(1)}, f32[2]{0:T(128)}, u32[]{:S(2)}) copy-start(f32[2]{0:T(128)} %uptake.1) | copy-start | bytes 28
  0.0 0.7 %copy-start.1 = (f32[2]{0:T(128)S(1)}, f32[2]{0:T(128)}, u32[]{:S(2)}) copy-start(f32[2]{0:T(128)} %diffusion.1) | copy-start | bytes 28
  0.7 0.7 %copy-start = (s32[4,6]{1,0:T(4,128)S(1)}, s32[4,6]{1,0:T(4,128)}, u32[]{:S(2)}) copy-start(s32[4,6]{1,0:T(4,128)} %nbr.1) | copy-start | bytes 292
